TPU v7x, 512 devices: a whole 4x8x8 slice. The times are simulated.
512 devices in a mesh: range: 16 (over y, core), date: 32 (over z, x).
Axes of the slice: x: 4, y: 8, z: 8, core: 2. Of those that a mesh axis runs over, the one named last changes fastest.
Arguments:
- slc: bfloat16 [2, 128, 128, 10240], P(None, 'date', None, 'range'), may hold values from -12 to 12
- row_offset: int32 [128], P('date'), may hold values from -16 to 15
- col_offset: int32 [128], P('date'), may hold values from -16 to 15
- valid: int32 [32, 512, 128], P('date', 'range'), may hold values 0 or 1
Outputs:
- coherence: bfloat16 [32, 512, 128, 128], P('date', 'range')
- pair_coherence: float32 [32, 512, 4, 2, 128], P('date', 'range')
Inputs may be any that keep to these rules, and one draw needn't show every extreme that they name: `row_offset`: offsets in eighths of a cell. `col_offset`: offsets in eighths of a cell.
All inputs are finite; a program needn't handle non-finite values. No bound on the sum of `valid` on one device may be relied on, other than what follows from the above.
Results may differ from a plain program's by a relative error of at most 0.0048.
Values may be sent and summed in bfloat16 or wider, within the bound.
A program may use at most 128 MiB of HBM per device.

v0:
```python
import jax
import jax.numpy as jnp
from jax import lax
from jax.sharding import PartitionSpec as P


def extended(block, sides, width):
    for axis, dim in sides:
        count = lax.axis_size(axis)
        forward = [(i, i + 1) for i in range(count - 1)]
        backward = [(target, source) for source, target in forward]
        low = lax.ppermute(
            lax.slice_in_dim(block, block.shape[dim] - width, None, axis=dim), axis, forward
        )
        high = lax.ppermute(lax.slice_in_dim(block, 0, width, axis=dim), axis, backward)
        block = jnp.concatenate([low, block, high], axis=dim)
    return block


def from_behind(value, axis, steps):
    count = lax.axis_size(axis)
    first, last = (max(0, -steps), min(count, count - steps))
    return lax.ppermute(value, axis, [(source, source + steps) for source in range(first, last)])


def lanczos(values):
    return jnp.where(jnp.abs(values) < 4.0, jnp.sinc(values) * jnp.sinc(values / 4.0), 0.0)


def tap_weights(offset):
    shift = offset.astype(jnp.float32) / 8.0
    taps = jnp.arange(-5, 6).astype(jnp.float32)
    return lanczos(shift[:, None] - taps[None, :]).astype(jnp.bfloat16)


def band_matrix(weights, inputs, outputs):
    inner = jnp.arange(inputs)[:, None] - jnp.arange(outputs)[None, :]
    matrix = jnp.zeros((weights.shape[0], inputs, outputs), jnp.bfloat16)
    for tap in range(11):
        select = jnp.where(inner == tap, 1.0, 0.0).astype(jnp.bfloat16)
        matrix = matrix + select[None] * weights[:, tap][:, None, None]
    return matrix


def block_size():
    return 128


def pixel_grams(block):
    width, dates, lines, items, looks = block.shape
    groups = lines // 4
    real_part = block[0].reshape(dates, groups, 4, items, looks)
    imag_part = block[1].reshape(dates, groups, 4, items, looks)

    def product(left, right):
        return jnp.einsum("dgaml,egaml->gmde", left, right, preferred_element_type=jnp.float32)

    count = float(4 * looks)
    cross_re = (product(real_part, real_part) + product(imag_part, imag_part)) / count
    cross_im = (product(imag_part, real_part) - product(real_part, imag_part)) / count
    scale = lax.rsqrt(jnp.diagonal(cross_re, axis1=2, axis2=3) + 1e-06)
    magnitude = (
        jnp.sqrt(cross_re * cross_re + cross_im * cross_im)
        * scale[..., :, None]
        * scale[..., None, :]
    )
    return magnitude


def pool_looks(values):
    dates, lines, cols = values.shape
    summed = values.reshape(dates, lines // 4, 4, cols // 20, 20).sum(axis=(2, 4)) / 80.0
    return summed.transpose(1, 2, 0)


def on_device(slc, row_offset, col_offset, valid):
    width, dates_here, lines, cols = slc.shape
    row_w = tap_weights(row_offset)
    col_w = tap_weights(col_offset)
    widened = extended(slc, (("range", 3),), 5)
    col_block = block_size()
    col_band = band_matrix(col_w, col_block + 10, col_block)
    windows = jnp.stack(
        [
            widened[..., start * col_block : start * col_block + col_block + 10]
            for start in range(cols // col_block)
        ],
        axis=3,
    )
    across = jnp.einsum("cdanp,dpk->cdank", windows, col_band, preferred_element_type=jnp.float32)
    across = across.reshape(width, dates_here, lines, cols).astype(jnp.bfloat16)
    row_block = block_size()
    row_band = band_matrix(row_w, row_block + 10, row_block)
    padded = jnp.pad(across, ((0, 0), (0, 0), (5, 5), (0, 0)))
    windows = jnp.stack([padded], axis=2)
    resampled = jnp.einsum(
        "cdnqk,dqr->cdnrk", windows, row_band, preferred_element_type=jnp.float32
    )
    resampled = resampled.reshape(width, dates_here, lines, cols).astype(jnp.bfloat16)
    looks = 20
    items = cols // looks
    blocks = resampled.reshape(width, dates_here, lines, items, looks)
    magnitude = (lambda block: pixel_grams(block))(
        lax.all_to_all(blocks, "date", split_axis=2, concat_axis=1, tiled=True)
    )
    later = from_behind(resampled, "date", -1)
    joined = jnp.concatenate([resampled, later], axis=1).astype(jnp.float32)
    real_all, imag_all = (joined[0], joined[1])
    power = pool_looks(real_all * real_all + imag_all * imag_all)
    scale_all = lax.rsqrt(power + 1e-06)
    near = scale_all[..., :dates_here]
    left_re, left_im = (real_all[:dates_here], imag_all[:dates_here])
    pair_list = []
    for step in range(1, 5):
        right_re, right_im = (
            real_all[step : step + dates_here],
            imag_all[step : step + dates_here],
        )
        real_pair = pool_looks(left_re * right_re + left_im * right_im)
        imag_pair = pool_looks(left_im * right_re - left_re * right_im)
        far = scale_all[..., step : step + dates_here]
        pair_list.append(jnp.stack([real_pair * near * far, imag_pair * near * far], axis=2))
    local_pairs = jnp.stack(pair_list, axis=2)
    pairs = lax.all_to_all(local_pairs, "date", split_axis=0, concat_axis=4, tiled=True)
    valid_f = valid.astype(jnp.float32)
    coherence = (magnitude * (valid_f[..., :, None] * valid_f[..., None, :])).astype(jnp.bfloat16)
    mask_list = []
    for step in range(1, 5):
        far_mask = jnp.pad(valid_f[..., step:], ((0, 0), (0, 0), (0, step)))
        mask_list.append(valid_f * far_mask)
    pair_masks = jnp.stack(mask_list, axis=2)
    pair_coherence = pairs * pair_masks[:, :, :, None, :]
    return (coherence, pair_coherence)


def solution(mesh):
    in_specs = (P(None, "date", None, "range"), P("date"), P("date"), P("date", "range", None))
    out_specs = (P("date", "range", None, None), P("date", "range", None, None, None))
    return jax.shard_map(
        on_device, mesh=mesh, in_specs=in_specs, out_specs=out_specs, check_vma=False
    )
```

profile of v0, /device:TPU:12, one launch (start us, length us, event | category | flops | bytes accessed | tf_op | source)
XLA Modules:
  0.0 326.9 jit_solution(18446410410665383027)
XLA Ops:
  4.4 3.6 %collective-permute-start.1 = (bf16[2,4,128,5]{2,3,0,1:T(8,128)(2,1)S(1)}, bf16[2,4,128,5]{2,3,0,1:T(8,128)(2,1)S(1)}, u32[]{:S(2)}, u32[]{:S(2)}) collective-permute-start(bf16[2,4,128,5]{2,3,0,1:T(8,128)(2,1)S(1)} %get-tuple-element.21), channel_id=1, source_target_pairs={{32,0},{64,32},{96,64},{128,96},{160,128},{192,160},{224,192},{256... | collective-permute-start | bytes 30728 | tf_op jit(solution)/shard_map/ppermute | solution.py:15
  14.7 30.4 %collective-permute-done.2 = bf16[2,4,128,640]{3,2,0,1:T(8,128)(2,1)S(1)} collective-permute-done((bf16[2,4,128,640]{3,2,0,1:T(8,128)(2,1)S(1)}, bf16[2,4,128,640]{3,2,0,1:T(8,128)(2,1)S(1)}, u32[]{:S(2)}, u32[]{:S(2)}) %collective-permute-start.2) | collective-permute-done | bytes 1310752 | tf_op jit(solution)/shard_map/ppermute | solution.py:23
  51.1 21.4 %add.238 = f32[8,32,4,32,20]{4,3,2,1,0:T(8,128)} reshape(f32[1,8,128,640]{3,2,0,1:T(8,128)S(1)} %fusion) | data formatting | bytes 5242880 | tf_op jit(solution)/shard_map/add | solution.py:109
  72.5 7.2 %reduce_sum.82 = f32[8,32,32]{2,1,0:T(8,128)S(1)} reduce(f32[8,32,4,32,20]{4,3,2,1,0:T(8,128)} %add.238, f32[]{:T(128)} %constant.48.clone.1), dimensions={2,4}, to_apply=%region_1.3 | reduce | flops 647168 | bytes 2654212 | tf_op jit(solution)/shard_map/reduce_sum | solution.py:72
  79.8 11.2 %add.236 = f32[4,32,4,32,20]{4,3,2,1,0:T(8,128)} reshape(f32[1,4,128,640]{3,2,0,1:T(8,128)S(1)} %copy-done.8) | data formatting | bytes 2621440 | tf_op jit(solution)/shard_map/add | solution.py:119
  90.9 4.2 %reduce_sum.81 = f32[4,32,32]{2,1,0:T(8,128)S(1)} reduce(f32[4,32,4,32,20]{4,3,2,1,0:T(8,128)} %add.236, f32[]{:T(128)} %constant.48.clone.1), dimensions={2,4}, to_apply=%region_0.2 | reduce | flops 323584 | bytes 1327108 | tf_op jit(solution)/shard_map/reduce_sum | solution.py:72
  95.1 11.2 %sub.272 = f32[4,32,4,32,20]{4,3,2,1,0:T(8,128)} reshape(f32[1,4,128,640]{3,2,0,1:T(8,128)S(1)} %copy-done.6) | data formatting | bytes 2621440 | tf_op jit(solution)/shard_map/sub | solution.py:120
  106.3 4.2 %reduce_sum.85 = f32[4,32,32]{2,1,0:T(8,128)S(1)} reduce(f32[4,32,4,32,20]{4,3,2,1,0:T(8,128)} %sub.272, f32[]{:T(128)} %constant.48.clone.1), dimensions={2,4}, to_apply=%region_4.6 | reduce | flops 323584 | bytes 1327108 | tf_op jit(solution)/shard_map/reduce_sum | solution.py:72
  110.5 11.2 %add.244 = f32[4,32,4,32,20]{4,3,2,1,0:T(8,128)} reshape(f32[1,4,128,640]{3,2,0,1:T(8,128)S(1)} %copy-done.7) | data formatting | bytes 2621440 | tf_op jit(solution)/shard_map/add | solution.py:119
  121.6 4.2 %reduce_sum.86 = f32[4,32,32]{2,1,0:T(8,128)S(1)} reduce(f32[4,32,4,32,20]{4,3,2,1,0:T(8,128)} %add.244, f32[]{:T(128)} %constant.48.clone.1), dimensions={2,4}, to_apply=%region_5.7 | reduce | flops 323584 | bytes 1327108 | tf_op jit(solution)/shard_map/reduce_sum | solution.py:72
  125.8 11.2 %sub.274 = f32[4,32,4,32,20]{4,3,2,1,0:T(8,128)} reshape(f32[1,4,128,640]{3,2,0,1:T(8,128)S(1)} %copy-done.4) | data formatting | bytes 2621440 | tf_op jit(solution)/shard_map/sub | solution.py:120
  137.0 4.2 %reduce_sum.87 = f32[4,32,32]{2,1,0:T(8,128)S(1)} reduce(f32[4,32,4,32,20]{4,3,2,1,0:T(8,128)} %sub.274, f32[]{:T(128)} %constant.48.clone.1), dimensions={2,4}, to_apply=%region_6.8 | reduce | flops 323584 | bytes 1327108 | tf_op jit(solution)/shard_map/reduce_sum | solution.py:72
  141.1 11.3 %add.246 = f32[4,32,4,32,20]{4,3,2,1,0:T(8,128)} reshape(f32[1,4,128,640]{3,2,0,1:T(8,128)S(1)} %copy-done.5) | data formatting | bytes 2621440 | tf_op jit(solution)/shard_map/add | solution.py:119
  152.5 4.2 %reduce_sum.88 = f32[4,32,32]{2,1,0:T(8,128)S(1)} reduce(f32[4,32,4,32,20]{4,3,2,1,0:T(8,128)} %add.246, f32[]{:T(128)} %constant.48.clone.1), dimensions={2,4}, to_apply=%region_7.9 | reduce | flops 323584 | bytes 1327108 | tf_op jit(solution)/shard_map/reduce_sum | solution.py:72
  156.6 11.2 %sub.276 = f32[4,32,4,32,20]{4,3,2,1,0:T(8,128)} reshape(f32[1,4,128,640]{3,2,0,1:T(8,128)S(1)} %copy-done.3) | data formatting | bytes 2621440 | tf_op jit(solution)/shard_map/sub | solution.py:120
  167.8 4.2 %reduce_sum.89 = f32[4,32,32]{2,1,0:T(8,128)S(1)} reduce(f32[4,32,4,32,20]{4,3,2,1,0:T(8,128)} %sub.276, f32[]{:T(128)} %constant.48.clone.1), dimensions={2,4}, to_apply=%region_8.10 | reduce | flops 323584 | bytes 1327108 | tf_op jit(solution)/shard_map/reduce_sum | solution.py:72
  172.0 11.2 %sub.270 = f32[4,32,4,32,20]{4,3,2,1,0:T(8,128)} reshape(f32[1,4,128,640]{3,2,0,1:T(8,128)S(1)} %copy-done.2) | data formatting | bytes 2621440 | tf_op jit(solution)/shard_map/sub | solution.py:120
  183.1 4.2 %reduce_sum.83 = f32[4,32,32]{2,1,0:T(8,128)S(1)} reduce(f32[4,32,4,32,20]{4,3,2,1,0:T(8,128)} %sub.270, f32[]{:T(128)} %constant.48.clone.1), dimensions={2,4}, to_apply=%region_2.4 | reduce | flops 323584 | bytes 1327108 | tf_op jit(solution)/shard_map/reduce_sum | solution.py:72
  187.3 11.2 %add.242 = f32[4,32,4,32,20]{4,3,2,1,0:T(8,128)} reshape(f32[1,4,128,640]{3,2,0,1:T(8,128)S(1)} %copy-done.1) | data formatting | bytes 2621440 | tf_op jit(solution)/shard_map/add | solution.py:119
  198.5 4.1 %reduce_sum.84 = f32[4,32,32]{2,1,0:T(8,128)S(1)} reduce(f32[4,32,4,32,20]{4,3,2,1,0:T(8,128)} %add.242, f32[]{:T(128)} %constant.48.clone.1), dimensions={2,4}, to_apply=%region_3.5 | reduce | flops 323584 | bytes 1327108 | tf_op jit(solution)/shard_map/reduce_sum | solution.py:72
  204.1 15.3 %all-to-all-start.1 = ((f32[32,1,1024]{2,1,0:T(1,128)}), f32[32,1,1024]{2,1,0:T(1,128)S(1)}, u32[]{:S(2)}, u32[]{:S(2)}) async-start(f32[32,1,1024]{2,1,0:T(1,128)} %reshape.367), calls=%async_computation.1 | async-start | bytes 262144 | tf_op jit(solution)/shard_map/all_to_all | solution.py:124
  221.0 7.1 %copy.108 = bf16[2,4,128,32,20]{3,1,4,0,2:T(4,128)(2,1)} copy(bf16[2,4,128,32,20]{2,1,4,3,0:T(4,128)(2,1)S(1)} %bitcast.276) | data formatting | bytes 2621440 | tf_op jit(solution)/shard_map/convert_element_type | solution.py:99
  228.0 9.0 %reshape.365 = bf16[32,2,10240]{2,1,0:T(2,128)(2,1)} reshape(bf16[128,2,20,4,32]{4,3,2,1,0:T(4,128)(2,1)} %bitcast.272) | data formatting | bytes 2621440
  237.0 10.2 %all-to-all-start = ((bf16[32,2,10240]{2,1,0:T(2,128)(2,1)}), bf16[32,2,10240]{2,1,0:T(2,128)(2,1)S(1)}, u32[]{:S(2)}, u32[]{:S(2)}) async-start(bf16[32,2,10240]{2,1,0:T(2,128)(2,1)} %reshape.365), calls=%async_computation | async-start | bytes 2621440 | tf_op jit(solution)/shard_map/all_to_all | solution.py:104
  250.5 30.4 %all-to-all-done = bf16[32,2,10240]{2,1,0:T(2,128)(2,1)S(1)} async-done(((bf16[32,2,10240]{2,1,0:T(2,128)(2,1)}), bf16[32,2,10240]{2,1,0:T(2,128)(2,1)S(1)}, u32[]{:S(2)}, u32[]{:S(2)}) %all-to-all-start) | async-done | bytes 1310752 | tf_op jit(solution)/shard_map/all_to_all | solution.py:104
  280.9 4.0 %reshape.366 = bf16[128,2,20,4,32]{4,3,2,1,0:T(4,128)(2,1)} reshape(bf16[32,2,10240]{2,1,0:T(2,128)(2,1)S(1)} %all-to-all-done) | data formatting | bytes 2621440
  284.9 4.5 %copy.109 = bf16[2,4,128,32,20]{3,2,4,1,0:T(8,128)(2,1)S(1)} copy(bf16[2,4,128,32,20]{3,1,4,0,2:T(4,128)(2,1)} %bitcast.273) | data formatting | bytes 2621440 | tf_op jit(solution)/shard_map/all_to_all | solution.py:104
  289.4 4.8 %fusion.227 = (bf16[1,32,4,4,32,20]{4,3,1,5,2,0:T(4,128)(2,1)S(1)}, bf16[1,32,4,4,32,20]{4,3,1,5,2,0:T(4,128)(2,1)S(1)}) fusion(bf16[2,32,4,4,32,20]{4,3,1,5,2,0:T(4,128)(2,1)S(1)} %bitcast.271), kind=kLoop, calls=%fused_computation.336 | loop fusion | bytes 2621440 | tf_op jit(solution)/shard_map/slice | solution.py:53
  294.2 3.5 %copy.110 = bf16[1,32,4,4,32,20]{4,2,1,5,3,0:T(4,128)(2,1)} copy(bf16[1,32,4,4,32,20]{4,3,1,5,2,0:T(4,128)(2,1)S(1)} %get-tuple-element.20) | data formatting | bytes 1310720 | tf_op jit(solution)/shard_map/slice | solution.py:52
  302.9 3.5 %copy.113 = bf16[1,32,4,4,32,20]{4,2,1,5,3,0:T(4,128)(2,1)} copy(bf16[1,32,4,4,32,20]{4,3,1,5,2,0:T(4,128)(2,1)S(1)} %get-tuple-element.19) | data formatting | bytes 1310720 | tf_op jit(solution)/shard_map/slice | solution.py:53
  313.7 6.3 %copy.120 = f32[32,128,128]{0,2,1:T(8,128)} copy(f32[32,128,128]{2,1,0:T(8,128)} %fusion.9) | data formatting | bytes 4194304 | tf_op jit(solution)/shard_map/div | solution.py:59
  321.9 4.8 %fusion.11 = bf16[1,32,128,128]{3,2,1,0:T(8,128)(2,1)} fusion(bf16[128,4,32,20]{0,3,1,2:T(8,128)(2,1)S(1)} %copy.111, bf16[128,4,32,20]{0,3,1,2:T(8,128)(2,1)S(1)} %copy.114, f32[32,128,128,1]{2,1,3,0:T(8,128)} %fusion.231, f32[32,128,128]{2,1,0:T(8,128)} %fusion.9, f32[32,128]{1,0:T(8,128)S(1)} %copy.121, f32[32,128]{1,0:T(8,128)S(1)} %get-tuple-element.36), kind=kOutput, calls=%fused_computation.19 | convolution fusion | flops 89128960 | bytes 6586368 | tf_op jit(solution)/shard_map/dgaml,egaml->gmde/dot_general | solution.py:56
  (93 shorter events, 36.7 us)
Async XLA Ops:
  0.6 7.6 %copy-start.13 = (s32[4]{0:T(128)S(1)}, s32[4]{0:T(128)}, u32[]{:S(2)}) copy-start(s32[4]{0:T(128)} %param.6) | copy-start | bytes 52
  0.6 7.6 %copy-start.12 = (s32[4]{0:T(128)S(1)}, s32[4]{0:T(128)}, u32[]{:S(2)}) copy-start(s32[4]{0:T(128)} %param.7) | copy-start | bytes 52
  2.5 6.0 %collective-permute-start = (bf16[2,4,128,5]{2,3,0,1:T(8,128)(2,1)S(1)}, bf16[2,4,128,5]{2,3,0,1:T(8,128)(2,1)S(1)}, u32[]{:S(2)}, u32[]{:S(2)}) collective-permute-start(bf16[2,4,128,5]{2,3,0,1:T(8,128)(2,1)S(1)} %get-tuple-element.22), channel_id=1, source_target_pairs={{0,32},{32,64},{64,96},{96,128},{128,160},{160,192},{192,224},{224... | collective-permute-start | bytes 30728 | tf_op jit(solution)/shard_map/ppermute | solution.py:12
  4.4 5.1 %collective-permute-start.1 = (bf16[2,4,128,5]{2,3,0,1:T(8,128)(2,1)S(1)}, bf16[2,4,128,5]{2,3,0,1:T(8,128)(2,1)S(1)}, u32[]{:S(2)}, u32[]{:S(2)}) collective-permute-start(bf16[2,4,128,5]{2,3,0,1:T(8,128)(2,1)S(1)} %get-tuple-element.21), channel_id=1, source_target_pairs={{32,0},{64,32},{96,64},{128,96},{160,128},{192,160},{224,192},{256... | collective-permute-start | bytes 30728 | tf_op jit(solution)/shard_map/ppermute | solution.py:15
  12.2 33.2 %copy-start.9 = (bf16[4,128,2,640]{3,1,2,0:T(8,128)(2,1)}, bf16[4,128,2,640]{3,1,2,0:T(8,128)(2,1)S(1)}, u32[]{:S(2)}) copy-start(bf16[4,128,2,640]{3,1,2,0:T(8,128)(2,1)S(1)} %convolution_convert_fusion) | copy-start | bytes 3932164
  12.2 32.9 %collective-permute-start.2 = (bf16[2,4,128,640]{3,2,0,1:T(8,128)(2,1)S(1)}, bf16[2,4,128,640]{3,2,0,1:T(8,128)(2,1)S(1)}, u32[]{:S(2)}, u32[]{:S(2)}) collective-permute-start(bf16[2,4,128,640]{3,2,0,1:T(8,128)(2,1)S(1)} %bitcast.277), channel_id=1, source_target_pairs={{1,0},{2,1},{3,2},{4,3},{5,4},{6,5},{7,6},{8,7},{9,8},{10,9},{11,1... | collective-permute-start | bytes 3932168 | tf_op jit(solution)/shard_map/ppermute | solution.py:23
  72.5 7.3 %copy-start.8 = (f32[1,4,128,640]{3,2,0,1:T(8,128)S(1)}, f32[1,4,128,640]{3,2,0,1:T(8,128)}, u32[]{:S(2)}) copy-start(f32[1,4,128,640]{3,2,0,1:T(8,128)} %get-tuple-element.11) | copy-start | bytes 3932164
  90.9 4.2 %copy-start.6 = (f32[1,4,128,640]{3,2,0,1:T(8,128)S(1)}, f32[1,4,128,640]{3,2,0,1:T(8,128)}, u32[]{:S(2)}) copy-start(f32[1,4,128,640]{3,2,0,1:T(8,128)} %get-tuple-element.14) | copy-start | bytes 3932164
  106.3 4.2 %copy-start.7 = (f32[1,4,128,640]{3,2,0,1:T(8,128)S(1)}, f32[1,4,128,640]{3,2,0,1:T(8,128)}, u32[]{:S(2)}) copy-start(f32[1,4,128,640]{3,2,0,1:T(8,128)} %get-tuple-element.18) | copy-start | bytes 3932164
  121.6 4.2 %copy-start.4 = (f32[1,4,128,640]{3,2,0,1:T(8,128)S(1)}, f32[1,4,128,640]{3,2,0,1:T(8,128)}, u32[]{:S(2)}) copy-start(f32[1,4,128,640]{3,2,0,1:T(8,128)} %get-tuple-element.12) | copy-start | bytes 3932164
  136.9 4.2 %copy-start.5 = (f32[1,4,128,640]{3,2,0,1:T(8,128)S(1)}, f32[1,4,128,640]{3,2,0,1:T(8,128)}, u32[]{:S(2)}) copy-start(f32[1,4,128,640]{3,2,0,1:T(8,128)} %get-tuple-element.16) | copy-start | bytes 3932164
  152.5 4.2 %copy-start.3 = (f32[1,4,128,640]{3,2,0,1:T(8,128)S(1)}, f32[1,4,128,640]{3,2,0,1:T(8,128)}, u32[]{:S(2)}) copy-start(f32[1,4,128,640]{3,2,0,1:T(8,128)} %get-tuple-element.17) | copy-start | bytes 3932164
  167.8 4.2 %copy-start.2 = (f32[1,4,128,640]{3,2,0,1:T(8,128)S(1)}, f32[1,4,128,640]{3,2,0,1:T(8,128)}, u32[]{:S(2)}) copy-start(f32[1,4,128,640]{3,2,0,1:T(8,128)} %get-tuple-element.15) | copy-start | bytes 3932164
  183.1 4.2 %copy-start.1 = (f32[1,4,128,640]{3,2,0,1:T(8,128)S(1)}, f32[1,4,128,640]{3,2,0,1:T(8,128)}, u32[]{:S(2)}) copy-start(f32[1,4,128,640]{3,2,0,1:T(8,128)} %get-tuple-element.13) | copy-start | bytes 3932164
  202.7 16.7 %copy-start.10 = (bf16[4,128,2,640]{3,1,2,0:T(8,128)(2,1)S(1)}, bf16[4,128,2,640]{3,1,2,0:T(8,128)(2,1)}, u32[]{:S(2)}) copy-start(bf16[4,128,2,640]{3,1,2,0:T(8,128)(2,1)} %copy-done.9) | copy-start | bytes 3932164
  204.1 32.9 %all-to-all-start.1 = ((f32[32,1,1024]{2,1,0:T(1,128)}), f32[32,1,1024]{2,1,0:T(1,128)S(1)}, u32[]{:S(2)}, u32[]{:S(2)}) async-start(f32[32,1,1024]{2,1,0:T(1,128)} %reshape.367), calls=%async_computation.1 | async-start | bytes 262144 | tf_op jit(solution)/shard_map/all_to_all | solution.py:124
  237.0 10.2 %copy-start.11 = (s32[1,32,128]{2,1,0:T(8,128)S(1)}, s32[1,32,128]{2,1,0:T(8,128)}, u32[]{:S(2)}) copy-start(s32[1,32,128]{2,1,0:T(8,128)} %param.8) | copy-start | bytes 49156
  237.0 43.9 %all-to-all-start = ((bf16[32,2,10240]{2,1,0:T(2,128)(2,1)}), bf16[32,2,10240]{2,1,0:T(2,128)(2,1)S(1)}, u32[]{:S(2)}, u32[]{:S(2)}) async-start(bf16[32,2,10240]{2,1,0:T(2,128)(2,1)} %reshape.365), calls=%async_computation | async-start | bytes 2621440 | tf_op jit(solution)/shard_map/all_to_all | solution.py:104
  310.0 1.9 copy-start
where the time goes:
time: 332 us; the launch traced here: 327 us
  local copies, waits for them, and re-layouts  170 us (51%)
  waiting for transfers between devices  61.4 us (18%)
  other arithmetic  48.1 us (14%)
  starting transfers between devices  33.5 us (10%)
  matrix products  12.2 us (4%)
    add x4, local copies, waits for them, and re-layouts, on_device(): real_pair = pool_looks(left_re * right_re + left_im * right_im)  44.8 us
    sub x4, local copies, waits for them, and re-layouts, on_device(): imag_pair = pool_looks(left_im * right_re - left_re * right_im)  44.7 us
    reduce_sum x9, other arithmetic, pool_looks(): values.reshape(dates, lines // 4, 4, cols // 20, 20).sum(axis=(2, 4)) / 80.0  40.4 us
    ppermute x1, waiting for transfers between devices, from_behind(): lax.ppermute(value, axis, [(source, source + steps) for source in range(f...  30.4 us
    all_to_all x1, waiting for transfers between devices, on_device(): lax.all_to_all(blocks, 'date', split_axis=2, concat_axis=1, tiled=True)  30.4 us
    add x1, local copies, waits for them, and re-layouts, on_device(): power = pool_looks(real_all * real_all + imag_all * imag_all)  21.4 us
    unnamed x37, local copies, waits for them, and re-layouts  17.2 us
    all_to_all x1, starting transfers between devices, on_device(): lax.all_to_all(local_pairs, 'date', split_axis=0, concat_axis=4, tiled=True)  15.3 us
  transfers between devices with their start and end apart: 5, of which 3 were waited for; matrix products, arithmetic and copies ran while one was open for 7% of the time, Pallas kernels for 0%

commit v1 on v0

v1 whole, which is shorter than its diff:
```python
import functools

import jax
import jax.numpy as jnp
from jax import lax
from jax.experimental import pallas as pl
from jax.experimental.pallas import tpu as pltpu
from jax.sharding import PartitionSpec as P

MESH = pl.DeviceIdType.MESH
PEERS = 32
RANGE = 16
LOOKS = 20
CHUNKS = ((1, 2, 3), (0,), (4,))


def sin_pi(r):
    q = r * r
    total = jnp.full_like(q, 0.000466302805767612)
    for c in (-0.00737043094571435, 0.0821458866111282, -0.599264529320792, 2.55016403987735, -5.16771278004997):
        total = total * q + c
    return r * (total * q + 3.14159265358979)


def sinc(x):
    whole = jnp.round(x)
    odd = whole - 2.0 * jnp.floor(whole * 0.5)
    value = sin_pi(x - whole) * (1.0 - 2.0 * odd)
    zero = x == 0.0
    return jnp.where(zero, 1.0, value / jnp.where(zero, 1.0, x * 3.14159265358979))


def lanczos(x):
    return jnp.where(jnp.abs(x) < 4.0, sinc(x) * sinc(x * 0.25), 0.0)


def iota(shape, dim):
    return lax.broadcasted_iota(jnp.int32, shape, dim)


def band_matrices(row_ref, col_ref, col_band, row_band):
    sub, lane = iota((8, 128), 0), iota((8, 128), 1)
    offset = jnp.zeros((8, 128), jnp.int32)
    for date in range(4):
        offset = jnp.where(sub == date, col_ref[date], offset)
        offset = jnp.where(sub == date + 4, row_ref[date], offset)
    place = jnp.where(lane >= 64, lane - 128, lane)
    tap = jnp.where(sub < 4, -place, place)
    weights = lanczos(offset.astype(jnp.float32) * 0.125 - tap.astype(jnp.float32))
    distance = iota((128, 128), 0) - iota((128, 128), 1)
    inside = jnp.abs(distance) <= 5
    rows = iota((128, 128), 0)
    lines = 4 * (rows % 32) + rows // 32
    line_inside = jnp.abs(lines - iota((128, 128), 1)) <= 5
    for date in range(4):
        line = jnp.broadcast_to(weights[date : date + 1], (8, 128))
        base = pltpu.roll(line, 0, 1, stride=1, stride_axis=0)
        ring = jnp.concatenate([base if b == 0 else pltpu.roll(base, 8 * b, 1) for b in range(16)], axis=0)
        col_band[date, :128] = jnp.where(inside, ring, 0.0).astype(jnp.bfloat16)
        col_band[date, 128:] = jnp.where(inside, 0.0, ring).astype(jnp.bfloat16)
        line = jnp.broadcast_to(weights[date + 4 : date + 5], (8, 128))
        base = pltpu.roll(line, 0, 1, stride=4, stride_axis=0)
        parts = []
        for a in range(4):
            for m in range(0, 32, 8):
                shift = 4 * m + a
                parts.append(base if shift == 0 else pltpu.roll(base, shift, 1))
        ring = jnp.concatenate(parts, axis=0)
        row_band[date] = jnp.where(line_inside, ring, 0.0).astype(jnp.bfloat16)


def resample(windows, slc, low, high, col_band, row_band, stage, send):
    low_lane = iota((128, 128), 1) < 64
    for date in range(4):
        left = []
        for window in windows:
            for part in range(2):
                def block(index):
                    return slc[part, date, :, index * 128 : index * 128 + 128]
                before = low[part, date] if window == 0 else block(window - 1)
                after = high[part, date] if window == 4 else block(window + 1)
                rim = jnp.where(low_lane, after, before)
                left.append(jnp.concatenate([block(window), rim], axis=1))
        left = jnp.concatenate(left, axis=0)
        across = jnp.dot(left, col_band[date], preferred_element_type=jnp.float32).astype(jnp.bfloat16)
        for spot in range(len(windows)):
            first = across[spot * 256 : spot * 256 + 128]
            second = across[spot * 256 + 128 : spot * 256 + 256]
            both = jnp.concatenate([first, second], axis=1)
            lines = jnp.dot(row_band[date], both, preferred_element_type=jnp.float32)
            for part in range(2):
                for a in range(4):
                    stage[spot, pl.ds(a * 8 + part * 4 + date, 32, stride=32), :] = lines[
                        a * 32 : a * 32 + 32, part * 128 : part * 128 + 128
                    ]
    for spot in range(len(windows)):
        send[:, :, spot * 128 : spot * 128 + 128] = (
            stage[spot].astype(jnp.bfloat16).reshape(PEERS, 32, 128)
        )


def gather_rows(spot, window, recv, stack):
    upper = iota((2, 4, 8, 128), 2) < 4
    for group in range(8):
        block = recv[4 * group : 4 * group + 4, :, spot * 128 : spot * 128 + 128]
        block = block.astype(jnp.float32).reshape(2, 2, 4, 8, 128)
        first, second = block[:, 0], block[:, 1]
        real = jnp.where(upper, first, pltpu.roll(second, 4, 2))
        imag = jnp.where(upper, pltpu.roll(first, 4, 2), second)
        for a in range(4):
            lanes = slice(a * 128, a * 128 + 128)
            stack[window, 16 * group : 16 * group + 16, lanes] = (
                real[:, a].reshape(16, 128).astype(jnp.bfloat16)
            )
            stack[window, 128 + 16 * group : 144 + 16 * group, lanes] = (
                imag[:, a].reshape(16, 128).astype(jnp.bfloat16)
            )


def pixel(index, windows, stack, valid, out, pair):
    gram = None
    lane = iota((1, 512), 1) % 128
    for window in windows:
        start = index * LOOKS - window * 128
        mask = jnp.where((lane >= start) & (lane < start + LOOKS), 1.0, 0.0).astype(jnp.bfloat16)
        rows = stack[window]
        term = lax.dot_general(
            rows * mask, rows, (((1,), (1,)), ((), ())), preferred_element_type=jnp.float32
        )
        gram = term if gram is None else gram + term
    real = gram[:128, :128] + gram[128:, 128:]
    imag = gram[128:, :128] - gram[:128, 128:]
    sub, col = iota((8, 128), 0), iota((8, 128), 1)
    block = (sub - col) >> 3
    step = (sub - col) & 7
    near_re = jnp.zeros((8, 128), jnp.float32)
    near_im = jnp.zeros((8, 128), jnp.float32)
    for b in range(16):
        near_re = jnp.where(block == -b, real[8 * b : 8 * b + 8], near_re)
        near_im = jnp.where(block == -b, imag[8 * b : 8 * b + 8], near_im)

    def diagonal(near, k):
        return jnp.sum(jnp.where(step == k, near, 0.0), axis=0, keepdims=True)

    power = diagonal(near_re, 0) + 8e-5
    mask = valid[pl.ds(index, 1), :].astype(jnp.float32)
    scale = lax.rsqrt(power) * mask
    square = scale * scale
    eye = iota((128, 128), 0) == iota((128, 128), 1)
    down = jnp.sum(jnp.where(eye, jnp.broadcast_to(square, (128, 128)), 0.0), axis=1, keepdims=True)
    value = (real * real + imag * imag) * square * down
    out[index] = jnp.where(value > 0.0, value * lax.rsqrt(value), 0.0).astype(jnp.bfloat16)
    pieces = []
    for k in range(1, 5):
        both = scale * pltpu.roll(scale, 128 - k, 1)
        pieces.append(diagonal(near_re, k) * both)
        pieces.append(-diagonal(near_im, k) * both)
    pair[index] = jnp.concatenate(pieces, axis=0)


def kernel(
    row_ref, col_ref, slc, valid, coherence, pair,
    low, high, col_band, row_band, stage, send_a, send_b, send_c, recv_a, recv_b, recv_c, stack, out,
    halo_sem, send_sem, recv_sem, own_sem, out_sem,
):
    date = lax.axis_index("date")
    spot = lax.axis_index("range")
    right = lax.rem(spot + 1, RANGE)
    left = lax.rem(spot + RANGE - 1, RANGE)
    barrier = pltpu.get_barrier_semaphore()
    for to in (left, right):
        pl.semaphore_signal(barrier, inc=1, device_id={"range": to}, device_id_type=MESH)

    def greet(step, carry):
        pl.semaphore_signal(
            barrier, inc=1, device_id={"date": lax.rem(date + step, PEERS)}, device_id_type=MESH
        )
        return carry

    lax.fori_loop(1, PEERS, greet, 0)
    band_matrices(row_ref, col_ref, col_band, row_band)
    sends, recvs = (send_a, send_b, send_c), (recv_a, recv_b, recv_c)
    resample(CHUNKS[0], slc, low, high, col_band, row_band, stage, send_a)
    pl.semaphore_wait(barrier, PEERS + 1)

    def launch(chunk):
        def one(step, carry):
            to = lax.rem(date + step, PEERS)
            pltpu.make_async_remote_copy(
                src_ref=sends[chunk].at[to],
                dst_ref=recvs[chunk].at[date],
                send_sem=send_sem.at[chunk],
                recv_sem=recv_sem.at[chunk],
                device_id={"date": to},
                device_id_type=MESH,
            ).start()
            return carry

        lax.fori_loop(1, PEERS, one, 0)
        pltpu.make_async_copy(sends[chunk].at[date], recvs[chunk].at[date], own_sem.at[chunk]).start()

    def landed(chunk):
        pltpu.make_async_copy(
            sends[chunk].at[date], recvs[chunk].at[date], own_sem.at[chunk]
        ).wait()
        some = recvs[chunk].at[pl.ds(0, PEERS - 1)]
        pltpu.make_async_copy(some, some, recv_sem.at[chunk]).wait()

    to_right = pltpu.make_async_remote_copy(
        src_ref=slc.at[:, :, :, pl.ds(512, 128)], dst_ref=low,
        send_sem=halo_sem.at[0], recv_sem=halo_sem.at[1],
        device_id={"range": right}, device_id_type=MESH,
    )
    to_left = pltpu.make_async_remote_copy(
        src_ref=slc.at[:, :, :, pl.ds(0, 128)], dst_ref=high,
        send_sem=halo_sem.at[2], recv_sem=halo_sem.at[3],
        device_id={"range": left}, device_id_type=MESH,
    )
    to_right.start()
    to_left.start()
    launch(0)
    to_right.wait()
    to_left.wait()

    @pl.when(spot == 0)
    def _():
        low[...] = jnp.zeros_like(low)

    @pl.when(spot == RANGE - 1)
    def _():
        high[...] = jnp.zeros_like(high)

    for chunk in (1, 2):
        resample(CHUNKS[chunk], slc, low, high, col_band, row_band, stage, sends[chunk])
        launch(chunk)

    def pixels(first, last, window):
        def one(index, carry):
            pixel(index, (window,), stack, valid, out, pair)
            return carry

        lax.fori_loop(first, last, one, 0)

    def store(first, last, slot):
        return pltpu.make_async_copy(
            out.at[pl.ds(first, last - first)], coherence.at[pl.ds(first, last - first)], out_sem.at[slot]
        )

    landed(0)
    for place, window in enumerate(CHUNKS[0]):
        gather_rows(place, window, recv_a, stack)
    pixels(7, 12, 1)
    pixel(12, (1, 2), stack, valid, out, pair)
    pixels(13, 19, 2)
    pixel(19, (2, 3), stack, valid, out, pair)
    pixels(20, 25, 3)
    store(7, 25, 0).start()
    landed(1)
    gather_rows(0, 0, recv_b, stack)
    pixels(0, 6, 0)
    pixel(6, (0, 1), stack, valid, out, pair)
    store(0, 7, 1).start()
    landed(2)
    gather_rows(0, 4, recv_c, stack)
    pixel(25, (3, 4), stack, valid, out, pair)
    pixels(26, 32, 4)
    store(25, 32, 2).start()
    for chunk in range(3):
        some = sends[chunk].at[pl.ds(0, PEERS - 1)]
        pltpu.make_async_copy(some, some, send_sem.at[chunk]).wait()
    store(7, 25, 0).wait()
    store(0, 7, 1).wait()
    store(25, 32, 2).wait()


def on_device(slc, row_offset, col_offset, valid):
    bf16 = jnp.bfloat16
    vmem = pl.BlockSpec(memory_space=pltpu.VMEM)
    smem = pl.BlockSpec(memory_space=pltpu.SMEM)
    blocks = [pltpu.VMEM((PEERS, 32, 128 * len(chunk)), bf16) for chunk in CHUNKS]
    coherence, pair = pl.pallas_call(
        kernel,
        out_shape=(
            jax.ShapeDtypeStruct((32, 128, 128), bf16),
            jax.ShapeDtypeStruct((32, 8, 128), jnp.float32),
        ),
        in_specs=[smem, smem, vmem, vmem],
        out_specs=(pl.BlockSpec(memory_space=pl.ANY), vmem),
        scratch_shapes=[
            pltpu.VMEM((2, 4, 128, 128), bf16),
            pltpu.VMEM((2, 4, 128, 128), bf16),
            pltpu.VMEM((4, 256, 128), bf16),
            pltpu.VMEM((4, 128, 128), bf16),
            pltpu.VMEM((3, 1024, 128), jnp.float32),
            *blocks,
            *blocks,
            pltpu.VMEM((5, 256, 512), bf16),
            pltpu.VMEM((32, 128, 128), bf16),
            pltpu.SemaphoreType.DMA((4,)),
            pltpu.SemaphoreType.DMA((3,)),
            pltpu.SemaphoreType.DMA((3,)),
            pltpu.SemaphoreType.DMA((3,)),
            pltpu.SemaphoreType.DMA((3,)),
        ],
        compiler_params=pltpu.CompilerParams(
            collective_id=0, has_side_effects=True, vmem_limit_bytes=48 << 20
        ),
    )(row_offset, col_offset, slc, valid[0])
    return coherence[None], pair.reshape(1, 32, 4, 2, 128)


def solution(mesh):
    in_specs = (P(None, "date", None, "range"), P("date"), P("date"), P("date", "range", None))
    out_specs = (P("date", "range", None, None), P("date", "range", None, None, None))
    return jax.shard_map(
        on_device, mesh=mesh, in_specs=in_specs, out_specs=out_specs, check_vma=False
    )
```

time: 332 us -> 54.7 us (0.16)
  the two profiles are of different devices: /device:TPU:12 before, /device:TPU:62 now
where the time goes in v1:
time: 54.7 us; the launch traced here: 54.5 us
  Pallas kernels  48.9 us (89%)
  local copies, waits for them, and re-layouts  4.96 us (9%)
  between operations  0.65 us (1%)
    pallas_call x1, Pallas kernels, on_device(): pl.pallas_call(kernel, out_shape=(jax.ShapeDtypeStruct((32, 128, 128), bf...  48.9 us
    unnamed x10, local copies, waits for them, and re-layouts  4.96 us

profile of v1, /device:TPU:62, one launch (start us, length us, event | category | flops | bytes accessed | tf_op | source)
XLA Modules:
  0.0 54.5 jit_solution(6333701135833283787)
XLA Ops:
  0.6 0.0 copy-start
  0.6 1.3 %copy-done = bf16[2,4,128,640]{3,2,1,0:T(8,128)(2,1)S(1)} copy-done((bf16[2,4,128,640]{3,2,1,0:T(8,128)(2,1)S(1)}, bf16[2,4,128,640]{3,2,1,0:T(8,128)(2,1)}, u32[]{:S(2)}) %copy-start) | copy-done | bytes 1310744
  1.9 0.0 copy-start.1
  1.9 0.7 %copy-done.1 = s32[1,32,128]{2,1,0:T(8,128)S(1)} copy-done((s32[1,32,128]{2,1,0:T(8,128)S(1)}, s32[1,32,128]{2,1,0:T(8,128)}, u32[]{:S(2)}) %copy-start.1) | copy-done | bytes 16408
  2.7 0.0 copy-start.2
  2.7 0.7 %copy-done.2 = s32[4]{0:T(128)S(1)} copy-done((s32[4]{0:T(128)S(1)}, s32[4]{0:T(128)}, u32[]{:S(2)}) %copy-start.2) | copy-done | bytes 40
  3.3 0.0 copy-start.3
  3.3 0.7 %copy-done.3 = s32[4]{0:T(128)S(1)} copy-done((s32[4]{0:T(128)S(1)}, s32[4]{0:T(128)}, u32[]{:S(2)}) %copy-start.3) | copy-done | bytes 40
  4.0 48.9 %shard_map.59 = (bf16[32,128,128]{2,1,0:T(8,128)(2,1)S(1)}, f32[32,8,128]{2,1,0:T(8,128)S(1)}) custom-call(s32[4]{0:T(128)S(1)} %copy-done.2, s32[4]{0:T(128)S(1)} %copy-done.3, bf16[2,4,128,640]{3,2,1,0:T(8,128)(2,1)S(1)} %copy-done, s32[32,128]{1,0:T(8,128)S(1)} %bitcast.5), custom_call_target="tpu_custom_call" | custom-call | tf_op jit(solution)/shard_map/pallas_call | solution.py:281
  52.9 1.0 %copy.8 = bf16[1,32,128,128]{3,2,1,0:T(8,128)(2,1)} copy(bf16[1,32,128,128]{3,2,1,0:T(8,128)(2,1)S(1)} %bitcast.3) | data formatting | bytes 2097152
  53.8 0.7 %copy.9 = f32[1,32,4,2,128]{4,3,2,1,0:T(2,128)} copy(f32[1,32,4,2,128]{4,3,2,1,0:T(2,128)S(1)} %bitcast.4) | data formatting | bytes 262144
Async XLA Ops:
  0.6 1.3 %copy-start = (bf16[2,4,128,640]{3,2,1,0:T(8,128)(2,1)S(1)}, bf16[2,4,128,640]{3,2,1,0:T(8,128)(2,1)}, u32[]{:S(2)}) copy-start(bf16[2,4,128,640]{3,2,1,0:T(8,128)(2,1)} %slc.1) | copy-start | bytes 3932164
  1.9 0.7 %copy-start.1 = (s32[1,32,128]{2,1,0:T(8,128)S(1)}, s32[1,32,128]{2,1,0:T(8,128)}, u32[]{:S(2)}) copy-start(s32[1,32,128]{2,1,0:T(8,128)} %param.7) | copy-start | bytes 49156
  2.7 0.7 %copy-start.2 = (s32[4]{0:T(128)S(1)}, s32[4]{0:T(128)}, u32[]{:S(2)}) copy-start(s32[4]{0:T(128)} %row_ref.1) | copy-start | bytes 52
  3.3 0.7 %copy-start.3 = (s32[4]{0:T(128)S(1)}, s32[4]{0:T(128)}, u32[]{:S(2)}) copy-start(s32[4]{0:T(128)} %col_ref.1) | copy-start | bytes 52

commit v2 on v1

--- a/solution.py
+++ b/solution.py
@@ -11,7 +11,7 @@
 PEERS = 32
 RANGE = 16
 LOOKS = 20
-CHUNKS = ((1, 2, 3), (0,), (4,))
+CHUNKS = ((1, 2, 3), (0, 4))
 
 
 def sin_pi(r):
@@ -155,13 +155,14 @@
         both = scale * pltpu.roll(scale, 128 - k, 1)
         pieces.append(diagonal(near_re, k) * both)
         pieces.append(-diagonal(near_im, k) * both)
-    pair[index] = jnp.concatenate(pieces, axis=0)
+    pair[index] = jnp.concatenate(pieces, axis=0).reshape(4, 2, 128)
 
 
 def kernel(
-    row_ref, col_ref, slc, valid, coherence, pair,
-    low, high, col_band, row_band, stage, send_a, send_b, send_c, recv_a, recv_b, recv_c, stack, out,
-    halo_sem, send_sem, recv_sem, own_sem, out_sem,
+    row_in, col_in, slc_in, valid_in, out, pair,
+    row_ref, col_ref, slc, valid, in_sem,
+    low, high, col_band, row_band, stage, send_a, send_b, recv_a, recv_b, stack,
+    halo_sem, send_sem, recv_sem, own_sem,
 ):
     date = lax.axis_index("date")
     spot = lax.axis_index("range")
@@ -178,25 +179,42 @@
         return carry
 
     lax.fori_loop(1, PEERS, greet, 0)
+    loads = [
+        pltpu.make_async_copy(source, target, in_sem.at[slot])
+        for slot, (source, target) in enumerate(
+            ((row_in, row_ref), (col_in, col_ref), (slc_in, slc), (valid_in, valid))
+        )
+    ]
+    for load in loads:
+        load.start()
+    loads[0].wait()
+    loads[1].wait()
     band_matrices(row_ref, col_ref, col_band, row_band)
-    sends, recvs = (send_a, send_b, send_c), (recv_a, recv_b, recv_c)
+    loads[2].wait()
+    loads[3].wait()
+    sends, recvs = (send_a, send_b), (recv_a, recv_b)
     resample(CHUNKS[0], slc, low, high, col_band, row_band, stage, send_a)
     pl.semaphore_wait(barrier, PEERS + 1)
 
     def launch(chunk):
         def one(step, carry):
-            to = lax.rem(date + step, PEERS)
-            pltpu.make_async_remote_copy(
-                src_ref=sends[chunk].at[to],
-                dst_ref=recvs[chunk].at[date],
-                send_sem=send_sem.at[chunk],
-                recv_sem=recv_sem.at[chunk],
-                device_id={"date": to},
-                device_id_type=MESH,
-            ).start()
+            pair_at = step // 4
+            to = (pair_at // 2 + 4 * (pair_at % 2)) * 4 + lax.rem(date + step, 4)
+
+            @pl.when(to != date)
+            def _():
+                pltpu.make_async_remote_copy(
+                    src_ref=sends[chunk].at[to],
+                    dst_ref=recvs[chunk].at[date],
+                    send_sem=send_sem.at[chunk],
+                    recv_sem=recv_sem.at[chunk],
+                    device_id={"date": to},
+                    device_id_type=MESH,
+                ).start()
+
             return carry
 
-        lax.fori_loop(1, PEERS, one, 0)
+        lax.fori_loop(0, PEERS, one, 0)
         pltpu.make_async_copy(sends[chunk].at[date], recvs[chunk].at[date], own_sem.at[chunk]).start()
 
     def landed(chunk):
@@ -230,21 +248,16 @@
     def _():
         high[...] = jnp.zeros_like(high)
 
-    for chunk in (1, 2):
-        resample(CHUNKS[chunk], slc, low, high, col_band, row_band, stage, sends[chunk])
-        launch(chunk)
+    resample(CHUNKS[1], slc, low, high, col_band, row_band, stage, send_b)
+    launch(1)
 
     def pixels(first, last, window):
         def one(index, carry):
             pixel(index, (window,), stack, valid, out, pair)
             return carry
 
-        lax.fori_loop(first, last, one, 0)
-
-    def store(first, last, slot):
-        return pltpu.make_async_copy(
-            out.at[pl.ds(first, last - first)], coherence.at[pl.ds(first, last - first)], out_sem.at[slot]
-        )
+        for index in range(first, last):
+            one(index, 0)
 
     landed(0)
     for place, window in enumerate(CHUNKS[0]):
@@ -254,39 +267,49 @@
     pixels(13, 19, 2)
     pixel(19, (2, 3), stack, valid, out, pair)
     pixels(20, 25, 3)
-    store(7, 25, 0).start()
     landed(1)
     gather_rows(0, 0, recv_b, stack)
+    gather_rows(1, 4, recv_b, stack)
     pixels(0, 6, 0)
     pixel(6, (0, 1), stack, valid, out, pair)
-    store(0, 7, 1).start()
-    landed(2)
-    gather_rows(0, 4, recv_c, stack)
     pixel(25, (3, 4), stack, valid, out, pair)
     pixels(26, 32, 4)
-    store(25, 32, 2).start()
-    for chunk in range(3):
+    for chunk in range(2):
         some = sends[chunk].at[pl.ds(0, PEERS - 1)]
         pltpu.make_async_copy(some, some, send_sem.at[chunk]).wait()
-    store(7, 25, 0).wait()
-    store(0, 7, 1).wait()
-    store(25, 32, 2).wait()
+
+
+def hand_over(coherence, pair, coherence_out, pair_out, sem):
+    copies = []
+    for part in range(4):
+        rows = pl.ds(part * 8, 8)
+        copies.append(pltpu.make_async_copy(coherence.at[rows], coherence_out.at[rows], sem.at[part]))
+    copies.append(pltpu.make_async_copy(pair, pair_out, sem.at[4]))
+    for copy in copies:
+        copy.start()
+    for copy in copies:
+        copy.wait()
 
 
 def on_device(slc, row_offset, col_offset, valid):
     bf16 = jnp.bfloat16
     vmem = pl.BlockSpec(memory_space=pltpu.VMEM)
-    smem = pl.BlockSpec(memory_space=pltpu.SMEM)
+    hbm = pl.BlockSpec(memory_space=pltpu.HBM)
     blocks = [pltpu.VMEM((PEERS, 32, 128 * len(chunk)), bf16) for chunk in CHUNKS]
     coherence, pair = pl.pallas_call(
         kernel,
         out_shape=(
-            jax.ShapeDtypeStruct((32, 128, 128), bf16),
-            jax.ShapeDtypeStruct((32, 8, 128), jnp.float32),
+            pltpu.VMEM((32, 128, 128), bf16),
+            pltpu.VMEM((32, 4, 2, 128), jnp.float32),
         ),
-        in_specs=[smem, smem, vmem, vmem],
-        out_specs=(pl.BlockSpec(memory_space=pl.ANY), vmem),
+        in_specs=[hbm, hbm, hbm, hbm],
+        out_specs=(vmem, vmem),
         scratch_shapes=[
+            pltpu.SMEM((4,), jnp.int32),
+            pltpu.SMEM((4,), jnp.int32),
+            pltpu.VMEM((2, 4, 128, 640), bf16),
+            pltpu.VMEM((32, 128), jnp.int32),
+            pltpu.SemaphoreType.DMA((4,)),
             pltpu.VMEM((2, 4, 128, 128), bf16),
             pltpu.VMEM((2, 4, 128, 128), bf16),
             pltpu.VMEM((4, 256, 128), bf16),
@@ -295,18 +318,28 @@
             *blocks,
             *blocks,
             pltpu.VMEM((5, 256, 512), bf16),
-            pltpu.VMEM((32, 128, 128), bf16),
             pltpu.SemaphoreType.DMA((4,)),
-            pltpu.SemaphoreType.DMA((3,)),
-            pltpu.SemaphoreType.DMA((3,)),
-            pltpu.SemaphoreType.DMA((3,)),
-            pltpu.SemaphoreType.DMA((3,)),
+            pltpu.SemaphoreType.DMA((2,)),
+            pltpu.SemaphoreType.DMA((2,)),
+            pltpu.SemaphoreType.DMA((2,)),
         ],
         compiler_params=pltpu.CompilerParams(
-            collective_id=0, has_side_effects=True, vmem_limit_bytes=48 << 20
+            collective_id=0, has_side_effects=True, vmem_limit_bytes=60 << 20
         ),
     )(row_offset, col_offset, slc, valid[0])
-    return coherence[None], pair.reshape(1, 32, 4, 2, 128)
+    hbm = pl.BlockSpec(memory_space=pltpu.HBM)
+    coherence, pair = pl.pallas_call(
+        hand_over,
+        out_shape=(
+            jax.ShapeDtypeStruct((32, 128, 128), bf16),
+            jax.ShapeDtypeStruct((32, 4, 2, 128), jnp.float32),
+        ),
+        in_specs=[vmem, vmem],
+        out_specs=(hbm, hbm),
+        scratch_shapes=[pltpu.SemaphoreType.DMA((5,))],
+        compiler_params=pltpu.CompilerParams(vmem_limit_bytes=4 << 20),
+    )(coherence, pair)
+    return coherence[None], pair[None]
 
 
 def solution(mesh):

time: 54.7 us -> 46.6 us (0.85)
  the two profiles are of different devices: /device:TPU:62 before, /device:TPU:137 now
where the time goes in v2:
time: 46.6 us; the launch traced here: 46.5 us
  Pallas kernels  45.8 us (98%)
  between operations  0.64 us (1%)
    pallas_call x1, Pallas kernels, on_device(): pl.pallas_call(kernel, out_shape=(pltpu.VMEM((32, 128, 128), bf16), pltpu...  44.8 us
    pallas_call x1, Pallas kernels, on_device(): pl.pallas_call(hand_over, out_shape=(jax.ShapeDtypeStruct((32, 128, 128),...  1.05 us

profile of v2, /device:TPU:137, one launch (start us, length us, event | category | flops | bytes accessed | tf_op | source)
XLA Modules:
  0.0 46.5 jit_solution(11498974502267876751)
XLA Ops:
  0.6 44.8 %shard_map.59 = (bf16[32,128,128]{2,1,0:T(8,128)(2,1)S(1)}, f32[32,4,2,128]{3,2,1,0:T(2,128)S(1)}) custom-call(s32[4]{0:T(128)} %row_in.1, s32[4]{0:T(128)} %col_in.1, bf16[2,4,128,640]{3,2,1,0:T(8,128)(2,1)} %slc_in.1, s32[32,128]{1,0:T(8,128)} %bitcast.3), custom_call_target="tpu_custom_call" | custom-call | tf_op jit(solution)/shard_map/pallas_call | solution.py:299
  45.4 1.0 %shard_map.60 = (bf16[32,128,128]{2,1,0:T(8,128)(2,1)}, f32[32,4,2,128]{3,2,1,0:T(2,128)}) custom-call(bf16[32,128,128]{2,1,0:T(8,128)(2,1)S(1)} %get-tuple-element.6.coherence, f32[32,4,2,128]{3,2,1,0:T(2,128)S(1)} %get-tuple-element.7.pair), custom_call_target="tpu_custom_call" | custom-call | tf_op jit(solution)/shard_map/pallas_call | solution.py:331

commit v3 on v2

--- a/solution.py
+++ b/solution.py
@@ -49,9 +49,8 @@
     weights = lanczos(offset.astype(jnp.float32) * 0.125 - tap.astype(jnp.float32))
     distance = iota((128, 128), 0) - iota((128, 128), 1)
     inside = jnp.abs(distance) <= 5
-    rows = iota((128, 128), 0)
-    lines = 4 * (rows % 32) + rows // 32
-    line_inside = jnp.abs(lines - iota((128, 128), 1)) <= 5
+    first = sub < 4
+    reach = [jnp.abs(lane - 4 * m - sub % 4) <= 5 for m in range(32)]
     for date in range(4):
         line = jnp.broadcast_to(weights[date : date + 1], (8, 128))
         base = pltpu.roll(line, 0, 1, stride=1, stride_axis=0)
@@ -59,71 +58,69 @@
         col_band[date, :128] = jnp.where(inside, ring, 0.0).astype(jnp.bfloat16)
         col_band[date, 128:] = jnp.where(inside, 0.0, ring).astype(jnp.bfloat16)
         line = jnp.broadcast_to(weights[date + 4 : date + 5], (8, 128))
-        base = pltpu.roll(line, 0, 1, stride=4, stride_axis=0)
-        parts = []
-        for a in range(4):
-            for m in range(0, 32, 8):
-                shift = 4 * m + a
-                parts.append(base if shift == 0 else pltpu.roll(base, shift, 1))
-        ring = jnp.concatenate(parts, axis=0)
-        row_band[date] = jnp.where(line_inside, ring, 0.0).astype(jnp.bfloat16)
-
-
-def resample(windows, slc, low, high, col_band, row_band, stage, send):
+        base = pltpu.roll(line, 0, 1, stride=1, stride_axis=0)
+        base = jnp.where(first, base, pltpu.roll(base, 124, 1))
+        real, imag = [], []
+        for m in range(32):
+            ring = base if m == 0 else pltpu.roll(base, 4 * m, 1)
+            real.append(jnp.where(reach[m] & first, ring, 0.0))
+            imag.append(jnp.where(reach[m] & ~first, ring, 0.0))
+        row_band[date, :, :128] = jnp.concatenate(real, axis=0).astype(jnp.bfloat16)
+        row_band[date, :, 128:] = jnp.concatenate(imag, axis=0).astype(jnp.bfloat16)
+
+
+def resample(windows, slc, low, high, col_band, row_band, send):
     low_lane = iota((128, 128), 1) < 64
-    for date in range(4):
-        left = []
-        for window in windows:
-            for part in range(2):
-                def block(index):
-                    return slc[part, date, :, index * 128 : index * 128 + 128]
-                before = low[part, date] if window == 0 else block(window - 1)
-                after = high[part, date] if window == 4 else block(window + 1)
-                rim = jnp.where(low_lane, after, before)
-                left.append(jnp.concatenate([block(window), rim], axis=1))
-        left = jnp.concatenate(left, axis=0)
-        across = jnp.dot(left, col_band[date], preferred_element_type=jnp.float32).astype(jnp.bfloat16)
-        for spot in range(len(windows)):
-            first = across[spot * 256 : spot * 256 + 128]
-            second = across[spot * 256 + 128 : spot * 256 + 256]
-            both = jnp.concatenate([first, second], axis=1)
-            lines = jnp.dot(row_band[date], both, preferred_element_type=jnp.float32)
-            for part in range(2):
-                for a in range(4):
-                    stage[spot, pl.ds(a * 8 + part * 4 + date, 32, stride=32), :] = lines[
-                        a * 32 : a * 32 + 32, part * 128 : part * 128 + 128
-                    ]
-    for spot in range(len(windows)):
-        send[:, :, spot * 128 : spot * 128 + 128] = (
-            stage[spot].astype(jnp.bfloat16).reshape(PEERS, 32, 128)
-        )
-
-
-def gather_rows(spot, window, recv, stack):
-    upper = iota((2, 4, 8, 128), 2) < 4
-    for group in range(8):
-        block = recv[4 * group : 4 * group + 4, :, spot * 128 : spot * 128 + 128]
-        block = block.astype(jnp.float32).reshape(2, 2, 4, 8, 128)
-        first, second = block[:, 0], block[:, 1]
-        real = jnp.where(upper, first, pltpu.roll(second, 4, 2))
-        imag = jnp.where(upper, pltpu.roll(first, 4, 2), second)
-        for a in range(4):
-            lanes = slice(a * 128, a * 128 + 128)
-            stack[window, 16 * group : 16 * group + 16, lanes] = (
-                real[:, a].reshape(16, 128).astype(jnp.bfloat16)
-            )
-            stack[window, 128 + 16 * group : 144 + 16 * group, lanes] = (
-                imag[:, a].reshape(16, 128).astype(jnp.bfloat16)
-            )
-
-
-def pixel(index, windows, stack, valid, out, pair):
+    count = len(windows)
+    for pair in range(2):
+        results = []
+        for date in (2 * pair, 2 * pair + 1):
+            left = []
+            for window in windows:
+                for part in range(2):
+                    def block(index):
+                        return slc[part, date, :, index * 128 : index * 128 + 128]
+                    before = low[part, date] if window == 0 else block(window - 1)
+                    after = high[part, date] if window == 4 else block(window + 1)
+                    rim = jnp.where(low_lane, after, before)
+                    left.append(jnp.concatenate([block(window), rim], axis=1))
+            left = jnp.concatenate(left, axis=0)
+            across = jnp.dot(left, col_band[date], preferred_element_type=jnp.float32).astype(jnp.bfloat16)
+            across = jnp.concatenate([across[i * 256 : i * 256 + 256] for i in range(count)], axis=1)
+            lines = jnp.dot(row_band[date], across, preferred_element_type=jnp.float32)
+            results.append(lines.reshape(PEERS, 8, 128 * count))
+        both = jnp.concatenate(results, axis=1)
+        send[:, 16 * pair : 16 * pair + 16, :] = both.astype(jnp.bfloat16)
+
+
+def gather_rows(windows, recv, swap, stack):
+    lanes = 128 * len(windows)
+    low = iota((64, 128), 1) < 64
+    for group in range(4):
+        block = recv[8 * group : 8 * group + 8].reshape(256, lanes)
+        rows = jnp.dot(swap[...], block, preferred_element_type=jnp.float32)
+        for place, window in enumerate(windows):
+            for pair in range(2):
+                first = rows[128 * pair : 128 * pair + 64, place * 128 : place * 128 + 128]
+                second = rows[128 * pair + 64 : 128 * pair + 128, place * 128 : place * 128 + 128]
+                second = pltpu.roll(second, 64, 1)
+                for half in range(2):
+                    mixed = jnp.where(low, second, first) if half else jnp.where(low, first, second)
+                    mixed = mixed.astype(jnp.bfloat16)
+                    for part in range(2):
+                        to = part * 128 + group * 32
+                        stack[2 * window + half, to : to + 32, pair * 128 : pair * 128 + 128] = mixed[
+                            part * 32 : part * 32 + 32
+                        ]
+
+
+def pixel(index, stack, valid, out, pair):
     gram = None
-    lane = iota((1, 512), 1) % 128
-    for window in windows:
-        start = index * LOOKS - window * 128
+    lane = iota((1, 256), 1) % 64
+    for half in range(index * LOOKS // 64, (index * LOOKS + LOOKS - 1) // 64 + 1):
+        start = index * LOOKS - half * 64
         mask = jnp.where((lane >= start) & (lane < start + LOOKS), 1.0, 0.0).astype(jnp.bfloat16)
-        rows = stack[window]
+        rows = stack[half]
         term = lax.dot_general(
             rows * mask, rows, (((1,), (1,)), ((), ())), preferred_element_type=jnp.float32
         )
@@ -161,7 +158,7 @@
 def kernel(
     row_in, col_in, slc_in, valid_in, out, pair,
     row_ref, col_ref, slc, valid, in_sem,
-    low, high, col_band, row_band, stage, send_a, send_b, recv_a, recv_b, stack,
+    low, high, col_band, row_band, swap, send_a, send_b, recv_a, recv_b, stack,
     halo_sem, send_sem, recv_sem, own_sem,
 ):
     date = lax.axis_index("date")
@@ -193,28 +190,29 @@
     loads[2].wait()
     loads[3].wait()
     sends, recvs = (send_a, send_b), (recv_a, recv_b)
-    resample(CHUNKS[0], slc, low, high, col_band, row_band, stage, send_a)
+    resample(CHUNKS[0], slc, low, high, col_band, row_band, send_a)
     pl.semaphore_wait(barrier, PEERS + 1)
 
     def launch(chunk):
-        def one(step, carry):
-            pair_at = step // 4
-            to = (pair_at // 2 + 4 * (pair_at % 2)) * 4 + lax.rem(date + step, 4)
-
-            @pl.when(to != date)
-            def _():
-                pltpu.make_async_remote_copy(
-                    src_ref=sends[chunk].at[to],
-                    dst_ref=recvs[chunk].at[date],
-                    send_sem=send_sem.at[chunk],
-                    recv_sem=recv_sem.at[chunk],
-                    device_id={"date": to},
-                    device_id_type=MESH,
-                ).start()
-
-            return carry
-
-        lax.fori_loop(0, PEERS, one, 0)
+        for z in (0, 1, 4, 2, 5, 3, 6, 7):
+
+            def one(step, carry):
+                to = z * 4 + (step ^ (step >> 1))
+
+                @pl.when(to != date)
+                def _():
+                    pltpu.make_async_remote_copy(
+                        src_ref=sends[chunk].at[to],
+                        dst_ref=recvs[chunk].at[date],
+                        send_sem=send_sem.at[chunk],
+                        recv_sem=recv_sem.at[chunk],
+                        device_id={"date": to},
+                        device_id_type=MESH,
+                    ).start()
+
+                return carry
+
+            lax.fori_loop(0, 4, one, 0)
         pltpu.make_async_copy(sends[chunk].at[date], recvs[chunk].at[date], own_sem.at[chunk]).start()
 
     def landed(chunk):
@@ -248,32 +246,23 @@
     def _():
         high[...] = jnp.zeros_like(high)
 
-    resample(CHUNKS[1], slc, low, high, col_band, row_band, stage, send_b)
+    resample(CHUNKS[1], slc, low, high, col_band, row_band, send_b)
     launch(1)
 
-    def pixels(first, last, window):
-        def one(index, carry):
-            pixel(index, (window,), stack, valid, out, pair)
-            return carry
-
+    def pixels(first, last):
         for index in range(first, last):
-            one(index, 0)
-
+            pixel(index, stack, valid, out, pair)
+
+    to_row, from_row = iota((256, 256), 0), iota((256, 256), 1)
+    source = (to_row % 32) * 8 + (to_row // 32) % 2 * 4 + to_row // 64
+    swap[...] = jnp.where(from_row == source, 1.0, 0.0).astype(jnp.bfloat16)
     landed(0)
-    for place, window in enumerate(CHUNKS[0]):
-        gather_rows(place, window, recv_a, stack)
-    pixels(7, 12, 1)
-    pixel(12, (1, 2), stack, valid, out, pair)
-    pixels(13, 19, 2)
-    pixel(19, (2, 3), stack, valid, out, pair)
-    pixels(20, 25, 3)
+    gather_rows(CHUNKS[0], recv_a, swap, stack)
+    pixels(7, 25)
     landed(1)
-    gather_rows(0, 0, recv_b, stack)
-    gather_rows(1, 4, recv_b, stack)
-    pixels(0, 6, 0)
-    pixel(6, (0, 1), stack, valid, out, pair)
-    pixel(25, (3, 4), stack, valid, out, pair)
-    pixels(26, 32, 4)
+    gather_rows(CHUNKS[1], recv_b, swap, stack)
+    pixels(0, 7)
+    pixels(25, 32)
     for chunk in range(2):
         some = sends[chunk].at[pl.ds(0, PEERS - 1)]
         pltpu.make_async_copy(some, some, send_sem.at[chunk]).wait()
@@ -313,11 +302,11 @@
             pltpu.VMEM((2, 4, 128, 128), bf16),
             pltpu.VMEM((2, 4, 128, 128), bf16),
             pltpu.VMEM((4, 256, 128), bf16),
-            pltpu.VMEM((4, 128, 128), bf16),
-            pltpu.VMEM((3, 1024, 128), jnp.float32),
+            pltpu.VMEM((4, 256, 256), bf16),
+            pltpu.VMEM((256, 256), bf16),
             *blocks,
             *blocks,
-            pltpu.VMEM((5, 256, 512), bf16),
+            pltpu.VMEM((10, 256, 256), bf16),
             pltpu.SemaphoreType.DMA((4,)),
             pltpu.SemaphoreType.DMA((2,)),
             pltpu.SemaphoreType.DMA((2,)),

time: 46.6 us -> 45.3 us (0.972)
  the two profiles are of different devices: /device:TPU:137 before, /device:TPU:185 now
where the time goes in v3:
time: 45.3 us; the launch traced here: 45.2 us
  Pallas kernels  44.6 us (98%)
  between operations  0.64 us (1%)
    pallas_call x1, Pallas kernels, on_device(): pl.pallas_call(kernel, out_shape=(pltpu.VMEM((32, 128, 128), bf16), pltpu...  43.5 us
    pallas_call x1, Pallas kernels, on_device(): pl.pallas_call(hand_over, out_shape=(jax.ShapeDtypeStruct((32, 128, 128),...  1.05 us

profile of v3, /device:TPU:185, one launch (start us, length us, event | category | flops | bytes accessed | tf_op | source)
XLA Modules:
  0.0 45.2 jit_solution(9799736715560250686)
XLA Ops:
  0.6 43.5 %shard_map.59 = (bf16[32,128,128]{2,1,0:T(8,128)(2,1)S(1)}, f32[32,4,2,128]{3,2,1,0:T(2,128)S(1)}) custom-call(s32[4]{0:T(128)} %row_in.1, s32[4]{0:T(128)} %col_in.1, bf16[2,4,128,640]{3,2,1,0:T(8,128)(2,1)} %slc_in.1, s32[32,128]{1,0:T(8,128)} %bitcast.3), custom_call_target="tpu_custom_call" | custom-call | tf_op jit(solution)/shard_map/pallas_call | solution.py:288
  44.1 1.0 %shard_map.60 = (bf16[32,128,128]{2,1,0:T(8,128)(2,1)}, f32[32,4,2,128]{3,2,1,0:T(2,128)}) custom-call(bf16[32,128,128]{2,1,0:T(8,128)(2,1)S(1)} %get-tuple-element.6.coherence, f32[32,4,2,128]{3,2,1,0:T(2,128)S(1)} %get-tuple-element.7.pair), custom_call_target="tpu_custom_call" | custom-call | tf_op jit(solution)/shard_map/pallas_call | solution.py:320

commit v4 on v3

--- a/solution.py
+++ b/solution.py
@@ -69,12 +69,14 @@
         row_band[date, :, 128:] = jnp.concatenate(imag, axis=0).astype(jnp.bfloat16)
 
 
-def resample(windows, slc, low, high, col_band, row_band, send):
+def resample(windows, slc, low, high, col_band, row_band, send, ready=None):
     low_lane = iota((128, 128), 1) < 64
     count = len(windows)
     for pair in range(2):
         results = []
         for date in (2 * pair, 2 * pair + 1):
+            if ready is not None:
+                ready[date].wait()
             left = []
             for window in windows:
                 for part in range(2):
@@ -179,7 +181,12 @@
     loads = [
         pltpu.make_async_copy(source, target, in_sem.at[slot])
         for slot, (source, target) in enumerate(
-            ((row_in, row_ref), (col_in, col_ref), (slc_in, slc), (valid_in, valid))
+            (
+                (row_in, row_ref),
+                (col_in, col_ref),
+                *((slc_in.at[:, each], slc.at[:, each]) for each in range(4)),
+                (valid_in, valid),
+            )
         )
     ]
     for load in loads:
@@ -187,10 +194,8 @@
     loads[0].wait()
     loads[1].wait()
     band_matrices(row_ref, col_ref, col_band, row_band)
-    loads[2].wait()
-    loads[3].wait()
     sends, recvs = (send_a, send_b), (recv_a, recv_b)
-    resample(CHUNKS[0], slc, low, high, col_band, row_band, send_a)
+    resample(CHUNKS[0], slc, low, high, col_band, row_band, send_a, loads[2:6])
     pl.semaphore_wait(barrier, PEERS + 1)
 
     def launch(chunk):
@@ -256,6 +261,7 @@
     to_row, from_row = iota((256, 256), 0), iota((256, 256), 1)
     source = (to_row % 32) * 8 + (to_row // 32) % 2 * 4 + to_row // 64
     swap[...] = jnp.where(from_row == source, 1.0, 0.0).astype(jnp.bfloat16)
+    loads[6].wait()
     landed(0)
     gather_rows(CHUNKS[0], recv_a, swap, stack)
     pixels(7, 25)
@@ -298,7 +304,7 @@
             pltpu.SMEM((4,), jnp.int32),
             pltpu.VMEM((2, 4, 128, 640), bf16),
             pltpu.VMEM((32, 128), jnp.int32),
-            pltpu.SemaphoreType.DMA((4,)),
+            pltpu.SemaphoreType.DMA((7,)),
             pltpu.VMEM((2, 4, 128, 128), bf16),
             pltpu.VMEM((2, 4, 128, 128), bf16),
             pltpu.VMEM((4, 256, 128), bf16),

time: 45.3 us -> 45.7 us (level)
  the two profiles are of different devices: /device:TPU:185 before, /device:TPU:169 now
where the time goes in v4:
time: 45.7 us; the launch traced here: 45.6 us
  Pallas kernels  44.9 us (98%)
  between operations  0.64 us (1%)
    pallas_call x1, Pallas kernels, on_device(): pl.pallas_call(kernel, out_shape=(pltpu.VMEM((32, 128, 128), bf16), pltpu...  43.9 us
    pallas_call x1, Pallas kernels, on_device(): pl.pallas_call(hand_over, out_shape=(jax.ShapeDtypeStruct((32, 128, 128),...  1.05 us

profile of v4, /device:TPU:169, one launch (start us, length us, event | category | flops | bytes accessed | tf_op | source)
XLA Modules:
  0.0 45.6 jit_solution(7488769967881672942)
XLA Ops:
  0.6 43.9 %shard_map.59 = (bf16[32,128,128]{2,1,0:T(8,128)(2,1)S(1)}, f32[32,4,2,128]{3,2,1,0:T(2,128)S(1)}) custom-call(s32[4]{0:T(128)} %row_in.1, s32[4]{0:T(128)} %col_in.1, bf16[2,4,128,640]{3,2,1,0:T(8,128)(2,1)} %slc_in.1, s32[32,128]{1,0:T(8,128)} %bitcast.3), custom_call_target="tpu_custom_call" | custom-call | tf_op jit(solution)/shard_map/pallas_call | solution.py:294
  44.5 1.0 %shard_map.60 = (bf16[32,128,128]{2,1,0:T(8,128)(2,1)}, f32[32,4,2,128]{3,2,1,0:T(2,128)}) custom-call(bf16[32,128,128]{2,1,0:T(8,128)(2,1)S(1)} %get-tuple-element.6.coherence, f32[32,4,2,128]{3,2,1,0:T(2,128)S(1)} %get-tuple-element.7.pair), custom_call_target="tpu_custom_call" | custom-call | tf_op jit(solution)/shard_map/pallas_call | solution.py:326

commit v5 on v3

--- a/solution.py
+++ b/solution.py
@@ -270,10 +270,10 @@
 
 def hand_over(coherence, pair, coherence_out, pair_out, sem):
     copies = []
-    for part in range(4):
-        rows = pl.ds(part * 8, 8)
+    for part in range(8):
+        rows = pl.ds(part * 4, 4)
         copies.append(pltpu.make_async_copy(coherence.at[rows], coherence_out.at[rows], sem.at[part]))
-    copies.append(pltpu.make_async_copy(pair, pair_out, sem.at[4]))
+    copies.append(pltpu.make_async_copy(pair, pair_out, sem.at[8]))
     for copy in copies:
         copy.start()
     for copy in copies:
@@ -325,7 +325,7 @@
         ),
         in_specs=[vmem, vmem],
         out_specs=(hbm, hbm),
-        scratch_shapes=[pltpu.SemaphoreType.DMA((5,))],
+        scratch_shapes=[pltpu.SemaphoreType.DMA((9,))],
         compiler_params=pltpu.CompilerParams(vmem_limit_bytes=4 << 20),
     )(coherence, pair)
     return coherence[None], pair[None]

time: 45.3 us -> 45.4 us (level)
  no operation moved by 1% of the time
where the time goes in v5:
time: 45.4 us; the launch traced here: 45.2 us
  Pallas kernels  44.6 us (98%)
  between operations  0.64 us (1%)
    pallas_call x1, Pallas kernels, on_device(): pl.pallas_call(kernel, out_shape=(pltpu.VMEM((32, 128, 128), bf16), pltpu...  43.5 us
    pallas_call x1, Pallas kernels, on_device(): pl.pallas_call(hand_over, out_shape=(jax.ShapeDtypeStruct((32, 128, 128),...  1.08 us

profile of v5, /device:TPU:185, one launch (start us, length us, event | category | flops | bytes accessed | tf_op | source)
XLA Modules:
  0.0 45.2 jit_solution(8074500783845061805)
XLA Ops:
  0.6 43.5 %shard_map.59 = (bf16[32,128,128]{2,1,0:T(8,128)(2,1)S(1)}, f32[32,4,2,128]{3,2,1,0:T(2,128)S(1)}) custom-call(s32[4]{0:T(128)} %row_in.1, s32[4]{0:T(128)} %col_in.1, bf16[2,4,128,640]{3,2,1,0:T(8,128)(2,1)} %slc_in.1, s32[32,128]{1,0:T(8,128)} %bitcast.3), custom_call_target="tpu_custom_call" | custom-call | tf_op jit(solution)/shard_map/pallas_call | solution.py:288
  44.1 1.1 %shard_map.60 = (bf16[32,128,128]{2,1,0:T(8,128)(2,1)}, f32[32,4,2,128]{3,2,1,0:T(2,128)}) custom-call(bf16[32,128,128]{2,1,0:T(8,128)(2,1)S(1)} %get-tuple-element.6.coherence, f32[32,4,2,128]{3,2,1,0:T(2,128)S(1)} %get-tuple-element.7.pair), custom_call_target="tpu_custom_call" | custom-call | tf_op jit(solution)/shard_map/pallas_call | solution.py:320
